TPU v7x, 768 devices: a whole 4x8x12 slice. The times are simulated.
768 devices in a mesh: rep: 96 (over x, z, core), shard: 8 (over y).
Axes of the slice: x: 4, y: 8, z: 12, core: 2. Of those that a mesh axis runs over, the one named last changes fastest.
Arguments:
- accumulated: bfloat16 [96, 3072, 3072], P('rep', None, 'shard'), may hold values from -12 to 12
- prior_right: bfloat16 [3072, 64], P('shard'), may hold values from -0.109375 to 0.109375
Outputs:
- update: bfloat16 [3072, 3072], P(None, 'shard')
- carried_error: bfloat16 [96, 3072, 3072], P('rep', None, 'shard')
All inputs are finite; a program needn't handle non-finite values.
Results may differ from a plain program's by a relative error of at most 0.0042.
Values sent between devices are 32-bit elements; how exact they have to be, the bound alone decides.
A program may use at most 32 MiB of HBM per device.

v0:
```python
import jax
import jax.numpy as jnp
from jax import lax
from jax.sharding import PartitionSpec as P


def orthonormal(left):
    gram = jnp.dot(
        left.T, left, precision=lax.Precision.HIGHEST, preferred_element_type=jnp.float32
    )
    factor = jnp.linalg.cholesky(gram)
    return jax.scipy.linalg.solve_triangular(factor, left.T, lower=True).T


def shards(accumulated, prior_right):
    block = accumulated[0]
    partial_left = jnp.dot(block, prior_right, preferred_element_type=jnp.float32)
    left = lax.psum(partial_left, ("rep", "shard"))
    basis = orthonormal(left)
    basis_low = basis.astype(jnp.bfloat16)
    partial_right = jnp.einsum("nm,nr->mr", block, basis_low, preferred_element_type=jnp.float32)
    right = lax.psum(partial_right, "rep") / lax.axis_size("rep")
    decoded = jnp.dot(
        basis, right.T, precision=lax.Precision.HIGHEST, preferred_element_type=jnp.float32
    )
    carried_error = (block.astype(jnp.float32) - decoded).astype(jnp.bfloat16)
    return (decoded.astype(jnp.bfloat16), carried_error[None])


def solution(mesh):
    placed = (P("rep", None, "shard"), P("shard", None))
    return jax.shard_map(
        shards,
        mesh=mesh,
        in_specs=placed,
        out_specs=(P(None, "shard"), P("rep", None, "shard")),
        check_vma=False,
    )
```

profile of v0, /device:TPU:1, one launch (start us, length us, event | category | flops | bytes accessed | tf_op | source)
XLA Modules:
  0.0 772.8 jit_solution(10194568304311029629)
XLA Ops:
  7.2 0.0 copy-start
  7.2 0.0 all-reduce.3.cloned.1.call-start
  7.2 0.7 copy-done
  8.0 3.4 fusion.3
  11.4 0.0 copy-start.1
  11.4 0.0 all-reduce.3.cloned.1.call-update
  11.4 0.0 all-reduce.5.cloned.1.call-start
  11.4 474.7 %all-reduce.3.cloned.1.call-done = f32[3072,64]{0,1:T(8,128)} async-done(((f32[3072,64]{0,1:T(8,128)}), f32[3072,64]{0,1:T(8,128)}) %all-reduce.3.cloned.1.call-update) | async-done | bytes 786448 | tf_op jit(solution)/shard_map/psum | solution.py:18
  486.1 2.1 fusion.19
  488.3 0.1 copy.4
  488.4 5.8 cholesky.16
  494.3 0.6 compare_reduce_fusion
  494.9 0.7 fusion.12
  495.6 4.9 custom-call.7
  500.5 2.0 fusion.13
  502.4 0.0 copy-done.1
  502.4 1.1 fusion.5
  503.5 0.0 all-reduce.5.cloned.1.call-update
  503.6 255.6 %all-reduce.5.cloned.1.call-done = f32[384,64]{0,1:T(8,128)} async-done(((f32[384,64]{0,1:T(8,128)}), f32[384,64]{0,1:T(8,128)}) %all-reduce.5.cloned.1.call-update) | async-done | bytes 98320 | tf_op jit(solution)/shard_map/psum | solution.py:22
  759.2 6.8 fusion
  (2 shorter events, 0.0 us)
Async XLA Ops:
  7.2 0.8 copy-start
  7.2 478.9 %all-reduce.3.cloned.1.call-start = ((), (), s32[]{:S(2)}) async-start(), calls=%async_computation | async-start | bytes 1572864 | tf_op jit(solution)/shard_map/psum | solution.py:18
  11.4 491.1 %copy-start.1 = (bf16[1,3072,384]{2,1,0:T(8,128)(2,1)S(1)}, bf16[1,3072,384]{2,1,0:T(8,128)(2,1)}, u32[]{:S(2)}) copy-start(bf16[1,3072,384]{2,1,0:T(8,128)(2,1)} %param.2) | copy-start | bytes 7077892
  11.4 747.8 %all-reduce.5.cloned.1.call-start = ((), (), s32[]{:S(2)}) async-start(), calls=%async_computation.1 | async-start | bytes 196608 | tf_op jit(solution)/shard_map/psum | solution.py:22
Sparse Core Ops, SparseCore 0:
  13.9 472.1 all-reduce.2
  503.7 255.4 all-reduce.4
where the time goes:
time: 773 us
  waiting for transfers between devices  730 us (94%)
  matrix products  15.4 us (2%)
  between operations  14.1 us (2%)
  other arithmetic  12.1 us (2%)
    psum x1, waiting for transfers between devices, shards(): left = lax.psum(partial_left, ('rep', 'shard'))  475 us
    psum x1, waiting for transfers between devices, shards(): right = lax.psum(partial_right, 'rep') / lax.axis_size('rep')  256 us
  transfers between devices with their start and end apart: 2, of which 2 were waited for; matrix products, arithmetic and copies ran while one was open for 0% of the time, Pallas kernels for 0%

commit v1 on v0

v1 whole, which is shorter than its diff:
```python
import functools

import jax
import jax.numpy as jnp
from jax import lax
from jax.experimental import pallas as pl
from jax.experimental.pallas import tpu as pltpu
from jax.sharding import PartitionSpec as P

MESH = pl.DeviceIdType.MESH
NX, NY, NZ, NC = 4, 8, 12, 2
REPS = NX * NZ * NC
RANK = 64
GROUP = RANK // (NX * NC)
HALF = RANK // NC
BLOCK = 384
COLS = 384
X_FAR = (2, 1, 3)
Y_FAR = (4, 3, 5, 2, 6, 1, 7)
Y_NEAR = (0, 1, 7, 2, 6, 3, 5, 4)
Z_FAR = (6, 5, 7, 4, 8, 3, 9, 2, 10, 1, 11)
XC_FAR = ((2, 1), (2, 0), (1, 1), (3, 1), (1, 0), (3, 0), (0, 1))
F32, BF16 = jnp.float32, jnp.bfloat16
NT = (((1,), (1,)), ((), ()))


def split3(value):
    high = value.astype(BF16)
    rest = value - high.astype(F32)
    middle = rest.astype(BF16)
    low = (rest - middle.astype(F32)).astype(BF16)
    return high, middle, low


def eliminate(tiles, first, last):
    tiles = list(tiles)
    rows = lax.broadcasted_iota(jnp.int32, (8, 1), 0)
    for k in range(first, last):
        own, at = divmod(k, 8)
        row = tiles[own][at : at + 1, :]
        scaled = row * (1.0 / row[:, k : k + 1])
        for i in range(own, 8):
            column = tiles[i][:, k : k + 1]
            if i == own:
                column = jnp.where(rows > at, column, 0.0)
            tiles[i] = tiles[i] - column * scaled
    return tiles


def exchange_kernel(
    pt_ref, a_ref, bk_ref, rk_ref,
    a_v, part, sib, half, xr, yb, yr, zr, left, racc, gacc, rpart, rr, zr2, rt, bk_v, w_v,
    a_sem, cs, cr, xs, xrs, ys, yrs, zs, zrs, ays, ayr, axs, axr, acs, acr,
    rs, rrs, z2s, z2r, qs, qr, bk_sem,
):
    rep, y = lax.axis_index("rep"), lax.axis_index("shard")
    x, z, c = rep // (NZ * NC), (rep // NC) % NZ, rep % NC

    def device(dx=0, dy=0, dz=0, dc=0):
        return (
            (((x + dx) % NX) * NZ + (z + dz) % NZ) * NC + (c + dc) % NC,
            (y + dy) % NY,
        )

    def send(src, dst, send_sem, recv_sem, where):
        return pltpu.make_async_remote_copy(
            src_ref=src, dst_ref=dst, send_sem=send_sem, recv_sem=recv_sem,
            device_id=where, device_id_type=MESH,
        )

    sent = []

    def start(copy):
        copy.start()
        sent.append(copy)

    barrier = pltpu.get_barrier_semaphore()
    partners = (
        [device(dz=o) for o in Z_FAR]
        + [device(dy=d) for d in Y_FAR]
        + [device(dx=ox, dc=oc) for ox, oc in XC_FAR]
    )
    for partner in partners:
        pl.semaphore_signal(barrier, inc=1, device_id=partner, device_id_type=MESH)

    rs_order = Y_FAR + (0,)
    a_copies = {}
    for d in rs_order:
        b = (y + d) % NY
        a_copies[d] = pltpu.make_async_copy(a_ref.at[b], a_v.at[b], a_sem.at[d])
        a_copies[d].start()

    group = c * NX + x
    mine = pl.ds(pl.multiple_of(group * GROUP, GROUP), GROUP)
    my_half = pl.ds(pl.multiple_of(c * HALF, HALF), HALF)
    its_half = pl.ds(pl.multiple_of((1 - c) * HALF, HALF), HALF)
    sibling = device(dc=1)

    def product(d):
        b = (y + d) % NY
        a_copies[d].wait()
        part[b] = lax.dot_general(pt_ref[...], a_v[b], NT, preferred_element_type=F32)

    def core_copy(d):
        b = (y + d) % NY
        return send(part.at[b, its_half], sib.at[b], cs.at[d], cr.at[d], sibling)

    def x_copy(i, d):
        o, b = X_FAR[i], (y + d) % NY
        rows = pl.ds(pl.multiple_of(((x + o) % NX) * GROUP, GROUP), GROUP)
        return send(half.at[b, rows], xr.at[i, b], xs.at[i, d], xrs.at[i, d], device(dx=o))

    def core_sum(d):
        b = (y + d) % NY
        core_copy(d).wait_recv()
        half[b] = part[b, my_half] + sib[b]
        for i in range(3):
            start(x_copy(i, d))

    product(rs_order[0])
    product(rs_order[1])
    pl.semaphore_wait(barrier, len(partners))
    start(core_copy(rs_order[0]))
    start(core_copy(rs_order[1]))
    for t in range(2, 8):
        product(rs_order[t])
        start(core_copy(rs_order[t]))
        core_sum(rs_order[t - 2])
    core_sum(rs_order[6])
    core_sum(rs_order[7])

    my_x = pl.ds(pl.multiple_of(x * GROUP, GROUP), GROUP)

    def y_copy(d):
        return send(yb.at[d], yr.at[d], ys.at[d], yrs.at[d], device(dy=d))

    for d in rs_order:
        b = (y + d) % NY
        for i in range(3):
            x_copy(i, d).wait_recv()
        yb[d] = half[b, my_x] + xr[0, b] + xr[1, b] + xr[2, b]
        if d:
            start(y_copy(d))
    total = yb[0]
    for d in (1, 7, 2, 6, 3, 5, 4):
        y_copy(d).wait_recv()
        total = total + yr[d]

    def z_copy(ref, send_sem, recv_sem, o):
        return send(ref.at[z], ref.at[z], send_sem.at[o], recv_sem.at[o], device(dz=o))

    def z_wait(ref, send_sem, recv_sem, o):
        at = ref.at[(z + NZ - o) % NZ]
        send(at, at, send_sem.at[o], recv_sem.at[o], device(dz=o)).wait_recv()

    def z_sum(ref):
        value = ref[0]
        for i in range(1, NZ):
            value = value + ref[i]
        return value

    zr[z] = total
    for o in Z_FAR:
        start(z_copy(zr, zs, zrs, o))
    for o in reversed(Z_FAR):
        z_wait(zr, zs, zrs, o)
    left[y, mine] = z_sum(zr)

    def ay_copy(d, at):
        ref = left.at[at, mine]
        return send(ref, ref, ays.at[d], ayr.at[d], device(dy=d))

    def ax_copy(i, d):
        ref = left.at[(y + NY - d) % NY, mine]
        return send(ref, ref, axs.at[i, d], axr.at[i, d], device(dx=X_FAR[i]))

    def ax_wait(i, d):
        theirs = c * NX + (x + NX - X_FAR[i]) % NX
        rows = pl.ds(pl.multiple_of(theirs * GROUP, GROUP), GROUP)
        ref = left.at[(y + NY - d) % NY, rows]
        send(ref, ref, axs.at[i, d], axr.at[i, d], device(dx=X_FAR[i])).wait_recv()

    def ac_copy(d):
        ref = left.at[(y + NY - d) % NY, my_half]
        return send(ref, ref, acs.at[d], acr.at[d], sibling)

    def ac_wait(d):
        ref = left.at[(y + NY - d) % NY, its_half]
        send(ref, ref, acs.at[d], acr.at[d], sibling).wait_recv()

    for d in Y_FAR:
        start(ay_copy(d, y))
    for d in Y_NEAR:
        if d:
            ay_copy(d, (y + NY - d) % NY).wait_recv()
        for i in range(3):
            start(ax_copy(i, d))

    def contract(d):
        b = (y + NY - d) % NY
        ac_wait(d)
        pieces = jnp.concatenate(split3(left[b]), axis=0)
        r = jnp.dot(pieces, a_v[b], preferred_element_type=F32)
        g = lax.dot_general(pieces, pieces, NT, preferred_element_type=F32)
        if d:
            racc[...] += r
            gacc[...] += g
        else:
            racc[...] = r
            gacc[...] = g

    for t, d in enumerate(Y_NEAR):
        for i in range(3):
            ax_wait(i, d)
        start(ac_copy(d))
        if t >= 2:
            contract(Y_NEAR[t - 2])
    contract(Y_NEAR[6])
    contract(Y_NEAR[7])

    rpart[...] = racc[0:64] + racc[64:128] + racc[128:192]

    def r_copy(i):
        ox, oc = XC_FAR[i]
        theirs = ((c + oc) % NC) * NX + (x + ox) % NX
        rows = pl.ds(pl.multiple_of(theirs * GROUP, GROUP), GROUP)
        return send(rpart.at[rows], rr.at[i], rs.at[i], rrs.at[i], device(dx=ox, dc=oc))

    for i in range(7):
        start(r_copy(i))

    one = gacc[0:64, 0:64]
    cross = gacc[0:64, 64:128] + gacc[64:128, 0:64]
    small = gacc[64:128, 64:128] + gacc[0:64, 128:192] + gacc[128:192, 0:64]
    gram = one + (cross + small)
    at_row = lax.broadcasted_iota(jnp.int32, (64, 64), 0)
    at_col = lax.broadcasted_iota(jnp.int32, (64, 64), 1)
    diagonal = at_row == at_col
    both = jnp.concatenate([gram, jnp.where(diagonal, 1.0, 0.0).astype(F32)], axis=1)
    tiles = eliminate([both[8 * i : 8 * i + 8] for i in range(8)], 0, 24)

    total = rpart[mine]
    for i in reversed(range(7)):
        r_copy(i).wait_recv()
        total = total + rr[i]
    zr2[z] = total
    for o in Z_FAR:
        start(z_copy(zr2, z2s, z2r, o))

    both = jnp.concatenate(eliminate(tiles, 24, 64), axis=0)
    scale = jnp.sum(jnp.where(diagonal, both[:, 0:64], 0.0), axis=1, keepdims=True)
    w_v[...] = both[:, 64:128] * (1.0 / jnp.sqrt(scale))

    for o in reversed(Z_FAR):
        z_wait(zr2, z2s, z2r, o)
    rt[mine] = z_sum(zr2)

    def q_copy(i):
        ox, oc = XC_FAR[i]
        ref = rt.at[mine]
        return send(ref, ref, qs.at[i], qr.at[i], device(dx=ox, dc=oc))

    def q_wait(i):
        ox, oc = XC_FAR[i]
        theirs = ((c + NC - oc) % NC) * NX + (x + NX - ox) % NX
        rows = pl.ds(pl.multiple_of(theirs * GROUP, GROUP), GROUP)
        ref = rt.at[rows]
        send(ref, ref, qs.at[i], qr.at[i], device(dx=ox, dc=oc)).wait_recv()

    for i in range(7):
        start(q_copy(i))

    for b in range(NY):
        basis_t = jnp.dot(
            w_v[...], left[b], precision=lax.Precision.HIGHEST, preferred_element_type=F32
        )
        high = basis_t.astype(BF16).astype(F32)
        low = basis_t - high
        packed = jnp.concatenate([high, high, low, low], axis=0)
        bk_v[b * BLOCK : (b + 1) * BLOCK] = packed.T.astype(BF16)
    out = pltpu.make_async_copy(bk_v, bk_ref, bk_sem)
    out.start()

    for i in reversed(range(7)):
        q_wait(i)
    right_t = jnp.dot(
        w_v[...], rt[...], precision=lax.Precision.HIGHEST, preferred_element_type=F32
    ) * (1.0 / REPS)
    high = right_t.astype(BF16)
    low = (right_t - high.astype(F32)).astype(BF16)
    rk_ref[...] = jnp.concatenate([high, low, high, low], axis=0)
    out.wait()
    for copy in sent:
        copy.wait_send()


def exchange(prior_t, blocks):
    dma = pltpu.SemaphoreType.DMA
    vmem = pltpu.VMEM
    return pl.pallas_call(
        exchange_kernel,
        out_shape=(
            jax.ShapeDtypeStruct((NY * BLOCK, 4 * RANK), BF16),
            jax.ShapeDtypeStruct((4 * RANK, COLS), BF16),
        ),
        in_specs=[
            pl.BlockSpec(memory_space=pltpu.VMEM),
            pl.BlockSpec(memory_space=pl.ANY),
        ],
        out_specs=(
            pl.BlockSpec(memory_space=pl.ANY),
            pl.BlockSpec(memory_space=pltpu.VMEM),
        ),
        scratch_shapes=[
            vmem((NY, BLOCK, COLS), BF16),
            vmem((NY, RANK, BLOCK), F32),
            vmem((NY, HALF, BLOCK), F32),
            vmem((NY, HALF, BLOCK), F32),
            vmem((3, NY, GROUP, BLOCK), F32),
            vmem((NY, GROUP, BLOCK), F32),
            vmem((NY, GROUP, BLOCK), F32),
            vmem((NZ, GROUP, BLOCK), F32),
            vmem((NY, RANK, BLOCK), F32),
            vmem((3 * RANK, COLS), F32),
            vmem((3 * RANK, 3 * RANK), F32),
            vmem((RANK, COLS), F32),
            vmem((7, GROUP, COLS), F32),
            vmem((NZ, GROUP, COLS), F32),
            vmem((RANK, COLS), F32),
            vmem((NY * BLOCK, 4 * RANK), BF16),
            vmem((RANK, RANK), F32),
            dma((8,)), dma((8,)), dma((8,)),
            dma((3, 8)), dma((3, 8)),
            dma((8,)), dma((8,)),
            dma((12,)), dma((12,)),
            dma((8,)), dma((8,)),
            dma((3, 8)), dma((3, 8)),
            dma((8,)), dma((8,)),
            dma((7,)), dma((7,)),
            dma((12,)), dma((12,)),
            dma((7,)), dma((7,)),
            dma,
        ],
        compiler_params=pltpu.CompilerParams(
            collective_id=0, has_side_effects=True, vmem_limit_bytes=32 * 2**20
        ),
        name="exchange",
    )(prior_t, blocks)


def finish_kernel(basis_ref, right_ref, a_ref, update_ref, error_ref):
    decoded = jnp.dot(basis_ref[...], right_ref[...], preferred_element_type=F32)
    update_ref[...] = decoded.astype(BF16)
    error_ref[...] = (a_ref[...].astype(F32) - decoded).astype(BF16)


def finish(basis, right, block):
    rows = 512
    tall = lambda width: pl.BlockSpec((rows, width), lambda i: (i, 0))
    shape = jax.ShapeDtypeStruct(block.shape, BF16)
    return pl.pallas_call(
        finish_kernel,
        grid=(block.shape[0] // rows,),
        out_shape=(shape, shape),
        in_specs=[
            tall(4 * RANK),
            pl.BlockSpec((4 * RANK, COLS), lambda i: (0, 0)),
            tall(COLS),
        ],
        out_specs=(tall(COLS), tall(COLS)),
        name="finish",
    )(basis, right, block)


def shards(accumulated, prior_right):
    block = accumulated[0]
    basis, right = exchange(prior_right.T, block.reshape(NY, BLOCK, COLS))
    update, error = finish(basis, right, block)
    return update, error[None]


def solution(mesh):
    placed = (P("rep", None, "shard"), P("shard", None))
    return jax.shard_map(
        shards,
        mesh=mesh,
        in_specs=placed,
        out_specs=(P(None, "shard"), P("rep", None, "shard")),
        check_vma=False,
    )
```

time: 773 us -> 81 us (0.10)
  waiting for transfers between devices: 730 us -> 0 us
  Pallas kernels: 0 us -> 75.7 us
  matrix products: 15.4 us -> 0 us
  between operations: 14.1 us -> 0.66 us
  other arithmetic: 12.1 us -> 0 us
    psum x2 -> x0, waiting for transfers between devices: 730 us -> none  [the longest x1 475 us: shards(): left = lax.psum(partial_left, ('rep', 'shard'))]
    pallas_call x0 -> x2, Pallas kernels: none -> 75.7 us  [the longest x1 69.2 us: exchange(): pl.pallas_call(exchange_kernel, out_shape=(jax.ShapeDtypeStruct((NY * BLO...]
    dot_general x4 -> x0, matrix products: 13.4 us -> none  [the longest x1 6.77 us: shards(): jnp.dot(basis, right.T, precision=lax.Precision.HIGHEST, preferred_elemen...]
    another operation x5 -> x0, other arithmetic: 12.1 us -> none  [the longest x3 6.52 us: orthonormal(): factor = jnp.linalg.cholesky(gram)]
  transfers between devices with their start and end apart: 2 -> 0, of which waited for: 2 -> 0; matrix products, arithmetic and copies ran while one was open for 0% -> 0% of each run, Pallas kernels for 0% -> 0%
where the time goes in v1:
time: 81 us; the launch traced here: 80.6 us
  Pallas kernels  75.7 us (93%)
  local copies, waits for them, and re-layouts  4.29 us (5%)
    pallas_call x1, Pallas kernels, exchange(): pl.pallas_call(exchange_kernel, out_shape=(jax.ShapeDtypeStruct((NY * BLO...  69.2 us
    pallas_call x1, Pallas kernels, finish(): pl.pallas_call(finish_kernel, grid=(block.shape[0] // rows,), out_shape=(...  6.47 us
    unnamed x8, local copies, waits for them, and re-layouts  4.29 us

profile of v1, /device:TPU:1, one launch (start us, length us, event | category | flops | bytes accessed | tf_op | source)
XLA Modules:
  0.0 80.6 jit_solution(7648632013243870580)
XLA Ops:
  0.6 0.0 copy-start
  0.6 1.7 %copy-done = bf16[1,3072,384]{2,1,0:T(8,128)(2,1)S(1)} copy-done((bf16[1,3072,384]{2,1,0:T(8,128)(2,1)S(1)}, bf16[1,3072,384]{2,1,0:T(8,128)(2,1)}, u32[]{:S(2)}) %copy-start) | copy-done | bytes 2359320
  2.3 0.0 copy-start.3
  2.3 0.8 copy-done.3
  3.1 69.2 %exchange.1 = (bf16[3072,256]{1,0:T(8,128)(2,1)S(1)}, bf16[256,384]{1,0:T(8,128)(2,1)S(1)}) custom-call(bf16[64,384]{1,0:T(8,128)(2,1)S(1)} %bitcast.6, bf16[8,384,384]{2,1,0:T(8,128)(2,1)S(1)} %bitcast.5), custom_call_target="tpu_custom_call" | custom-call | tf_op jit(solution)/shard_map/exchange/pallas_call | solution.py:300
  72.3 0.0 copy-start.1
  72.3 1.1 %copy-done.1 = bf16[3072,256]{1,0:T(8,128)(2,1)} copy-done((bf16[3072,256]{1,0:T(8,128)(2,1)}, bf16[3072,256]{1,0:T(8,128)(2,1)S(1)}, u32[]{:S(2)}) %copy-start.1) | copy-done | bytes 1572888
  73.5 0.0 copy-start.2
  73.5 0.7 copy-done.2
  74.1 6.5 %finish.1 = (bf16[3072,384]{1,0:T(8,128)(2,1)}, bf16[3072,384]{1,0:T(8,128)(2,1)}) custom-call(bf16[3072,256]{1,0:T(8,128)(2,1)} %copy-done.1, bf16[256,384]{1,0:T(8,128)(2,1)} %copy-done.2, bf16[3072,384]{1,0:T(8,128)(2,1)} %bitcast.4), custom_call_target="tpu_custom_call" | custom-call | tf_op jit(solution)/shard_map/finish/pallas_call | solution.py:361
Async XLA Ops:
  0.6 1.7 %copy-start = (bf16[1,3072,384]{2,1,0:T(8,128)(2,1)S(1)}, bf16[1,3072,384]{2,1,0:T(8,128)(2,1)}, u32[]{:S(2)}) copy-start(bf16[1,3072,384]{2,1,0:T(8,128)(2,1)} %param.2) | copy-start | bytes 7077892
  2.3 0.8 copy-start.3
  72.3 1.2 %copy-start.1 = (bf16[3072,256]{1,0:T(8,128)(2,1)}, bf16[3072,256]{1,0:T(8,128)(2,1)S(1)}, u32[]{:S(2)}) copy-start(bf16[3072,256]{1,0:T(8,128)(2,1)S(1)} %get-tuple-element.6.basis_ref) | copy-start | bytes 4718596
  73.5 0.7 copy-start.2

commit v2 on v1

v2 whole, which is shorter than its diff:
```python
import functools

import jax
import jax.numpy as jnp
from jax import lax
from jax.experimental import pallas as pl
from jax.experimental.pallas import tpu as pltpu
from jax.sharding import PartitionSpec as P

MESH = pl.DeviceIdType.MESH
NX, NY, NZ, NC = 4, 8, 12, 2
REPS = NX * NZ * NC
RANK = 64
GROUP = RANK // (NX * NC)
HALF = RANK // NC
BLOCK = 384
COLS = 384
X_FAR = (2, 1, 3)
Y_FAR = (4, 3, 5, 2, 6, 1, 7)
Y_NEAR = (0, 1, 7, 2, 6, 3, 5, 4)
LAST = 4
Z_FAR = (6, 5, 7, 4, 8, 3, 9, 2, 10, 1, 11)
XC_FAR = ((2, 1), (2, 0), (1, 1), (3, 1), (1, 0), (3, 0), (0, 1))
EXCHANGE_VMEM = int(49.95 * 2**20)
F32, BF16 = jnp.float32, jnp.bfloat16
NT = (((1,), (1,)), ((), ()))


def split3(value):
    high = value.astype(BF16)
    rest = value - high.astype(F32)
    middle = rest.astype(BF16)
    low = (rest - middle.astype(F32)).astype(BF16)
    return high, middle, low


def eliminate(tiles, first, last):
    tiles = list(tiles)
    rows = lax.broadcasted_iota(jnp.int32, (8, 1), 0)
    for k in range(first, last):
        own, at = divmod(k, 8)
        row = tiles[own][at : at + 1, :]
        scaled = row * (1.0 / row[:, k : k + 1])
        for i in range(own, 8):
            column = tiles[i][:, k : k + 1]
            if i == own:
                column = jnp.where(rows > at, column, 0.0)
            tiles[i] = tiles[i] - column * scaled
    return tiles


def exchange_kernel(
    pt_ref, a_ref, bk_ref, rk_ref, a_v,
    pt_v, part, sib, half, xr, yb, yr, zr, left, racc, gacc, rpart, rr, zr2, rt, both_v, w_v,
    pt_sem, a_sem, cs, cr, xs, xrs, ys, yrs, zs, zrs, ays, ayr, axs, axr, als, alr, acs, acr,
    rs, rrs, z2s, z2r, qs, qr,
):
    rep, y = lax.axis_index("rep"), lax.axis_index("shard")
    chip = lax.div(rep, NC)
    x, z, c = lax.div(chip, NZ), lax.rem(chip, NZ), lax.rem(rep, NC)

    @functools.cache
    def device(dx=0, dy=0, dz=0, dc=0):
        return (
            (lax.rem(x + dx, NX) * NZ + lax.rem(z + dz, NZ)) * NC + lax.rem(c + dc, NC),
            lax.rem(y + dy, NY),
        )

    @functools.cache
    def block_at(d):
        return lax.rem(y + NY + d, NY)

    @functools.cache
    def group_rows(dx, dc):
        theirs = lax.rem(c + NC + dc, NC) * NX + lax.rem(x + NX + dx, NX)
        return pl.ds(pl.multiple_of(theirs * GROUP, GROUP), GROUP)

    def send(src, dst, send_sem, recv_sem, where):
        return pltpu.make_async_remote_copy(
            src_ref=src, dst_ref=dst, send_sem=send_sem, recv_sem=recv_sem,
            device_id=where, device_id_type=MESH,
        )

    sent = []

    def start(copy):
        copy.start()
        sent.append(copy)

    def drain(count):
        for copy in sent[:count]:
            copy.wait_send()
        del sent[:count]

    barrier = pltpu.get_barrier_semaphore()
    partners = (
        [device(dz=o) for o in Z_FAR]
        + [device(dy=d) for d in Y_FAR]
        + [device(dx=ox, dc=oc) for ox, oc in XC_FAR]
    )
    for partner in partners:
        pl.semaphore_signal(barrier, inc=1, device_id=partner, device_id_type=MESH)

    pt_copy = pltpu.make_async_copy(pt_ref, pt_v, pt_sem)
    pt_copy.start()
    rs_order = Y_FAR + (0,)
    a_copies = {}
    for d in rs_order:
        b = block_at(d)
        a_copies[d] = pltpu.make_async_copy(a_ref.at[b], a_v.at[b], a_sem.at[d])
        a_copies[d].start()

    mine = group_rows(0, 0)
    my_half = pl.ds(pl.multiple_of(c * HALF, HALF), HALF)
    its_half = pl.ds(pl.multiple_of((1 - c) * HALF, HALF), HALF)
    sibling = device(dc=1)

    def product(d):
        b = block_at(d)
        a_copies[d].wait()
        part[b] = lax.dot_general(pt_v[...], a_v[b], NT, preferred_element_type=F32)

    def core_copy(d):
        b = block_at(d)
        return send(part.at[b, its_half], sib.at[b], cs.at[d], cr.at[d], sibling)

    def x_copy(i, d):
        o, b = X_FAR[i], block_at(d)
        rows = pl.ds(pl.multiple_of(lax.rem(x + o, NX) * GROUP, GROUP), GROUP)
        return send(half.at[b, rows], xr.at[i, b], xs.at[i, d], xrs.at[i, d], device(dx=o))

    def core_sum(d):
        b = block_at(d)
        core_copy(d).wait_recv()
        half[b] = part[b, my_half] + sib[b]
        for i in range(3):
            start(x_copy(i, d))

    pt_copy.wait()
    for d in rs_order:
        product(d)
    pl.semaphore_wait(barrier, len(partners))
    for d in rs_order:
        start(core_copy(d))
    for d in rs_order:
        core_sum(d)

    my_x = pl.ds(pl.multiple_of(x * GROUP, GROUP), GROUP)

    def y_copy(d):
        return send(yb.at[d], yr.at[d], ys.at[d], yrs.at[d], device(dy=d))

    for d in rs_order:
        b = block_at(d)
        for i in range(3):
            x_copy(i, d).wait_recv()
        yb[d] = half[b, my_x] + xr[0, b] + xr[1, b] + xr[2, b]
        if d:
            start(y_copy(d))
    total = yb[0]
    for d in (1, 7, 2, 6, 3, 5, 4):
        y_copy(d).wait_recv()
        total = total + yr[d]

    def z_copy(ref, send_sem, recv_sem, o):
        return send(ref.at[z], ref.at[z], send_sem.at[o], recv_sem.at[o], device(dz=o))

    def z_wait(ref, send_sem, recv_sem, o):
        at = ref.at[lax.rem(z + NZ - o, NZ)]
        send(at, at, send_sem.at[o], recv_sem.at[o], device(dz=o)).wait_recv()

    def z_sum(ref):
        value = ref[0]
        for i in range(1, NZ):
            value = value + ref[i]
        return value

    zr[z] = total
    for o in Z_FAR:
        start(z_copy(zr, zs, zrs, o))
    drain(len(sent) - len(Z_FAR))
    for o in reversed(Z_FAR):
        z_wait(zr, zs, zrs, o)
    left[y, mine] = z_sum(zr)

    def ay_copy(d, at):
        ref = left.at[at, mine]
        return send(ref, ref, ays.at[d], ayr.at[d], device(dy=d))

    def ax_copy(i, d):
        ref = left.at[block_at(-d), mine]
        return send(ref, ref, axs.at[i, d], axr.at[i, d], device(dx=X_FAR[i]))

    def ax_wait(i, d):
        ref = left.at[block_at(-d), group_rows(-X_FAR[i], 0)]
        send(ref, ref, axs.at[i, d], axr.at[i, d], device(dx=X_FAR[i])).wait_recv()

    def ac_copy(d):
        ref = left.at[block_at(-d), my_half]
        return send(ref, ref, acs.at[d], acr.at[d], sibling)

    def ac_wait(d):
        ref = left.at[block_at(-d), its_half]
        send(ref, ref, acs.at[d], acr.at[d], sibling).wait_recv()

    def al_copy(i):
        ox, oc = XC_FAR[i]
        ref = left.at[block_at(-LAST), mine]
        return send(ref, ref, als.at[i], alr.at[i], device(dx=ox, dc=oc))

    def al_wait(i):
        ox, oc = XC_FAR[i]
        ref = left.at[block_at(-LAST), group_rows(-ox, -oc)]
        send(ref, ref, als.at[i], alr.at[i], device(dx=ox, dc=oc)).wait_recv()

    for d in Y_FAR:
        start(ay_copy(d, y))
    for d in Y_NEAR:
        if d:
            ay_copy(d, block_at(-d)).wait_recv()
        if d == LAST:
            for i in range(7):
                start(al_copy(i))
        else:
            for i in range(3):
                start(ax_copy(i, d))

    def contract(d):
        b = block_at(-d)
        if d == LAST:
            for i in range(7):
                al_wait(i)
        else:
            ac_wait(d)
        pieces = jnp.concatenate(split3(left[b]), axis=0)
        r = jnp.dot(pieces, a_v[b], preferred_element_type=F32)
        g = lax.dot_general(pieces, pieces, NT, preferred_element_type=F32)
        if d:
            racc[...] += r
            gacc[...] += g
        else:
            racc[...] = r
            gacc[...] = g

    for t, d in enumerate(Y_NEAR[:-1]):
        for i in range(3):
            ax_wait(i, d)
        start(ac_copy(d))
        if t >= 2:
            contract(Y_NEAR[t - 2])
    for d in Y_NEAR[5:]:
        contract(d)

    rpart[...] = racc[0:64] + racc[64:128] + racc[128:192]

    def r_copy(i):
        ox, oc = XC_FAR[i]
        return send(rpart.at[group_rows(ox, oc)], rr.at[i], rs.at[i], rrs.at[i], device(dx=ox, dc=oc))

    for i in range(7):
        start(r_copy(i))

    def apart(body):
        pl.when(rep >= 0)(body)

    at_row = lax.broadcasted_iota(jnp.int32, (64, 64), 0)
    at_col = lax.broadcasted_iota(jnp.int32, (64, 64), 1)
    diagonal = at_row == at_col

    def steps(first, last):
        tiles = eliminate([both_v[8 * i : 8 * i + 8] for i in range(8)], first, last)
        for i in range(first // 8, 8):
            both_v[8 * i : 8 * i + 8] = tiles[i]

    @apart
    def _():
        one = gacc[0:64, 0:64]
        cross = gacc[0:64, 64:128] + gacc[64:128, 0:64]
        small = gacc[64:128, 64:128] + gacc[0:64, 128:192] + gacc[128:192, 0:64]
        gram = one + (cross + small)
        unit = jnp.where(diagonal, 1.0, 0.0).astype(F32)
        both_v[...] = jnp.concatenate([gram, unit], axis=1)
        steps(0, 16)

    total = rpart[mine]
    for i in reversed(range(7)):
        r_copy(i).wait_recv()
        total = total + rr[i]
    zr2[z] = total
    for o in Z_FAR:
        start(z_copy(zr2, z2s, z2r, o))

    @apart
    def _():
        steps(16, 64)
        both = both_v[...]
        scale = jnp.sum(jnp.where(diagonal, both[:, 0:64], 0.0), axis=1, keepdims=True)
        w_v[...] = both[:, 64:128] * (1.0 / jnp.sqrt(scale))

    drain(len(sent) - len(Z_FAR))
    for o in reversed(Z_FAR):
        z_wait(zr2, z2s, z2r, o)
    rt[mine] = z_sum(zr2)

    def q_copy(i):
        ox, oc = XC_FAR[i]
        ref = rt.at[mine]
        return send(ref, ref, qs.at[i], qr.at[i], device(dx=ox, dc=oc))

    def q_wait(i):
        ox, oc = XC_FAR[i]
        ref = rt.at[group_rows(-ox, -oc)]
        send(ref, ref, qs.at[i], qr.at[i], device(dx=ox, dc=oc)).wait_recv()

    for i in range(7):
        start(q_copy(i))

    @apart
    def _():
        for b in range(NY):
            basis_t = jnp.dot(
                w_v[...], left[b], precision=lax.Precision.HIGHEST, preferred_element_type=F32
            )
            high = basis_t.astype(BF16).astype(F32)
            low = basis_t - high
            packed = jnp.concatenate([high, high, low, low], axis=0)
            bk_ref[b * BLOCK : (b + 1) * BLOCK] = packed.T.astype(BF16)

    drain(len(sent) - len(XC_FAR))
    for i in reversed(range(7)):
        q_wait(i)
    right_t = jnp.dot(
        w_v[...], rt[...], precision=lax.Precision.HIGHEST, preferred_element_type=F32
    ) * (1.0 / REPS)
    high = right_t.astype(BF16)
    low = (right_t - high.astype(F32)).astype(BF16)
    rk_ref[...] = jnp.concatenate([high, low, high, low], axis=0)
    drain(len(sent))


def exchange(prior_t, blocks):
    dma = pltpu.SemaphoreType.DMA
    vmem = pltpu.VMEM
    return pl.pallas_call(
        exchange_kernel,
        out_shape=(
            jax.ShapeDtypeStruct((NY * BLOCK, 4 * RANK), BF16),
            jax.ShapeDtypeStruct((4 * RANK, COLS), BF16),
            jax.ShapeDtypeStruct((NY, BLOCK, COLS), BF16),
        ),
        in_specs=[pl.BlockSpec(memory_space=pltpu.HBM)] * 2,
        out_specs=(pl.BlockSpec(memory_space=pltpu.VMEM),) * 3,
        scratch_shapes=[
            vmem((RANK, BLOCK), BF16),
            vmem((NY, RANK, BLOCK), F32),
            vmem((NY, HALF, BLOCK), F32),
            vmem((NY, HALF, BLOCK), F32),
            vmem((3, NY, GROUP, BLOCK), F32),
            vmem((NY, GROUP, BLOCK), F32),
            vmem((NY, GROUP, BLOCK), F32),
            vmem((NZ, GROUP, BLOCK), F32),
            vmem((NY, RANK, BLOCK), F32),
            vmem((3 * RANK, COLS), F32),
            vmem((3 * RANK, 3 * RANK), F32),
            vmem((RANK, COLS), F32),
            vmem((7, GROUP, COLS), F32),
            vmem((NZ, GROUP, COLS), F32),
            vmem((RANK, COLS), F32),
            vmem((RANK, 2 * RANK), F32),
            vmem((RANK, RANK), F32),
            dma, dma((8,)), dma((8,)), dma((8,)),
            dma((3, 8)), dma((3, 8)),
            dma((8,)), dma((8,)),
            dma((12,)), dma((12,)),
            dma((8,)), dma((8,)),
            dma((3, 8)), dma((3, 8)),
            dma((7,)), dma((7,)),
            dma((8,)), dma((8,)),
            dma((7,)), dma((7,)),
            dma((12,)), dma((12,)),
            dma((7,)), dma((7,)),
        ],
        compiler_params=pltpu.CompilerParams(
            collective_id=0, has_side_effects=True, vmem_limit_bytes=EXCHANGE_VMEM
        ),
        name="exchange",
    )(prior_t, blocks)


def finish_kernel(basis_ref, right_ref, a_ref, update_ref, error_ref, up, er, up_sem, er_sem):
    copies = []
    for b in range(NY):
        decoded = jnp.dot(
            basis_ref[b * BLOCK : (b + 1) * BLOCK], right_ref[...], preferred_element_type=F32
        )
        up[b] = decoded.astype(BF16)
        copies.append(pltpu.make_async_copy(up.at[b], update_ref.at[b], up_sem.at[b]))
        copies[-1].start()
        er[b] = (a_ref[b].astype(F32) - decoded).astype(BF16)
        copies.append(pltpu.make_async_copy(er.at[b], error_ref.at[b], er_sem.at[b]))
        copies[-1].start()
    for copy in copies:
        copy.wait()


def finish(basis, right, blocks):
    shape = jax.ShapeDtypeStruct(blocks.shape, BF16)
    return pl.pallas_call(
        finish_kernel,
        out_shape=(shape, shape),
        in_specs=[pl.BlockSpec(memory_space=pltpu.VMEM)] * 3,
        out_specs=(pl.BlockSpec(memory_space=pl.ANY),) * 2,
        scratch_shapes=[
            pltpu.VMEM((NY, BLOCK, COLS), BF16),
            pltpu.VMEM((NY, BLOCK, COLS), BF16),
            pltpu.SemaphoreType.DMA((NY,)),
            pltpu.SemaphoreType.DMA((NY,)),
        ],
        compiler_params=pltpu.CompilerParams(vmem_limit_bytes=16 * 2**20),
        name="finish",
    )(basis, right, blocks)


def shards(accumulated, prior_right):
    block = accumulated[0]
    basis, right, held = exchange(prior_right.T, block.reshape(NY, BLOCK, COLS))
    update, error = finish(basis, right, held)
    return update.reshape(block.shape), error.reshape(accumulated.shape)


def solution(mesh):
    placed = (P("rep", None, "shard"), P("shard", None))
    return jax.shard_map(
        shards,
        mesh=mesh,
        in_specs=placed,
        out_specs=(P(None, "shard"), P("rep", None, "shard")),
        check_vma=False,
    )
```

time: 81 us -> 69.8 us (0.86)
  Pallas kernels: 75.7 us -> 68.1 us
  local copies, waits for them, and re-layouts: 4.29 us -> 0.79 us
    pallas_call x1, Pallas kernels: 6.47 us -> 2.58 us  [finish(): pl.pallas_call(finish_kernel, out_shape=(shape, shape), in_specs=[pl.Bloc...]
    pallas_call x1, Pallas kernels: 69.2 us -> 65.6 us  [exchange(): pl.pallas_call(exchange_kernel, out_shape=(jax.ShapeDtypeStruct((NY * BLO...]
    unnamed x8 -> x2, local copies, waits for them, and re-layouts: 4.29 us -> 0.79 us
where the time goes in v2:
time: 69.8 us; the launch traced here: 69.6 us
  Pallas kernels  68.1 us (98%)
  local copies, waits for them, and re-layouts  0.79 us (1%)
    pallas_call x1, Pallas kernels, exchange(): pl.pallas_call(exchange_kernel, out_shape=(jax.ShapeDtypeStruct((NY * BLO...  65.6 us
    pallas_call x1, Pallas kernels, finish(): pl.pallas_call(finish_kernel, out_shape=(shape, shape), in_specs=[pl.Bloc...  2.58 us

profile of v2, /device:TPU:1, one launch (start us, length us, event | category | flops | bytes accessed | tf_op | source)
XLA Modules:
  0.0 69.6 jit_solution(13957415107576286916)
XLA Ops:
  0.6 0.0 copy-start
  0.6 0.8 %copy-done = bf16[384,64]{0,1:T(8,128)(2,1)S(1)} copy-done((bf16[384,64]{0,1:T(8,128)(2,1)S(1)}, bf16[384,64]{0,1:T(8,128)(2,1)}, u32[]{:S(2)}) %copy-start) | copy-done | bytes 49176
  1.4 65.6 %exchange.1 = (bf16[3072,256]{1,0:T(8,128)(2,1)S(1)}, bf16[256,384]{1,0:T(8,128)(2,1)S(1)}, bf16[8,384,384]{2,1,0:T(8,128)(2,1)S(1)}) custom-call(bf16[64,384]{1,0:T(8,128)(2,1)S(1)} %bitcast.4, bf16[8,384,384]{2,1,0:T(8,128)(2,1)} %bitcast.5), custom_call_target="tpu_custom_call" | custom-call | tf_op jit(solution)/shard_map/exchange/pallas_call | solution.py:344
  67.0 2.6 %finish.1 = (bf16[8,384,384]{2,1,0:T(8,128)(2,1)}, bf16[8,384,384]{2,1,0:T(8,128)(2,1)}) custom-call(bf16[3072,256]{1,0:T(8,128)(2,1)S(1)} %get-tuple-element.7.basis_ref, bf16[256,384]{1,0:T(8,128)(2,1)S(1)} %get-tuple-element.8.right_ref, bf16[8,384,384]{2,1,0:T(8,128)(2,1)S(1)} %get-tuple-element.9.a_ref), custom_call_target="tpu_custom_call" | custom-call | tf_op jit(solution)/shard_map/finish/pallas_call | solution.py:408
Async XLA Ops:
  0.6 0.8 %copy-start = (bf16[384,64]{0,1:T(8,128)(2,1)S(1)}, bf16[384,64]{0,1:T(8,128)(2,1)}, u32[]{:S(2)}) copy-start(bf16[384,64]{0,1:T(8,128)(2,1)} %param.3) | copy-start | bytes 147460

commit v3 on v2

v3 whole, which is shorter than its diff:
```python
import functools

import jax
import jax.numpy as jnp
from jax import lax
from jax.experimental import pallas as pl
from jax.experimental.pallas import tpu as pltpu
from jax.sharding import PartitionSpec as P

MESH = pl.DeviceIdType.MESH
NX, NY, NZ, NC = 4, 8, 12, 2
REPS = NX * NZ * NC
RANK = 64
GROUP = RANK // (NX * NC)
HALF = RANK // NC
BLOCK = 384
COLS = 384
X_FAR = (2, 1, 3)
Y_FAR = (4, 3, 5, 2, 6, 1, 7)
RS_ORDER = Y_FAR + (0,)
RS_GROUPS = ((0, 1), (1, 2), (3, 2), (5, 3))
AG_ORDER = (0, 1, 7, 2, 6, 3, 5, 4)
AG_GROUPS = ((0, 3), (3, 2), (5, 2), (7, 1))
AG_GROUP_OF = (0, 0, 0, 1, 1, 2, 2, 3)
Z_FAR = (6, 5, 7, 4, 8, 3, 9, 2, 10, 1, 11)
XC_FAR = ((2, 1), (2, 0), (1, 1), (3, 1), (1, 0), (3, 0), (0, 1))
EXCHANGE_VMEM = int(49.95 * 2**20)
F32, BF16 = jnp.float32, jnp.bfloat16
NT = (((1,), (1,)), ((), ()))


def split3(value):
    high = value.astype(BF16)
    rest = value - high.astype(F32)
    middle = rest.astype(BF16)
    low = (rest - middle.astype(F32)).astype(BF16)
    return high, middle, low


def eliminate(tiles, first, last):
    tiles = list(tiles)
    rows = lax.broadcasted_iota(jnp.int32, (8, 1), 0)
    for k in range(first, last):
        own, at = divmod(k, 8)
        row = tiles[own][at : at + 1, :]
        scaled = row * (1.0 / row[:, k : k + 1])
        for i in range(own, 8):
            column = tiles[i][:, k : k + 1]
            if i == own:
                column = jnp.where(rows > at, column, 0.0)
            tiles[i] = tiles[i] - column * scaled
    return tiles


def exchange_kernel(
    pt_ref, a_ref, bk_ref, rk_ref, a_v,
    pt_v, part, sib, half, xr, yb, yr, zr, left, racc, gacc, rpart, rr, zr2, rt, both_v, w_v,
    pt_sem, a_sem, cs, cr, xs, xrs, ys, yrs, zs, zrs, ays, ayr, axs, axr, acs, acr,
    rs, rrs, z2s, z2r, qs, qr,
):
    rep, y = lax.axis_index("rep"), lax.axis_index("shard")
    chip = lax.div(rep, NC)
    x, z, c = lax.div(chip, NZ), lax.rem(chip, NZ), lax.rem(rep, NC)

    @functools.cache
    def device(dx=0, dy=0, dz=0, dc=0):
        return (
            (lax.rem(x + dx, NX) * NZ + lax.rem(z + dz, NZ)) * NC + lax.rem(c + dc, NC),
            lax.rem(y + dy, NY),
        )

    ahead = [lax.rem(y + d, NY) for d in range(NY)]
    behind = [lax.rem(y + NY - d, NY) for d in range(NY)]

    def group_rows(dx, dc):
        theirs = lax.rem(c + dc, NC) * NX + lax.rem(x + dx, NX)
        return pl.ds(pl.multiple_of(theirs * GROUP, GROUP), GROUP)

    def send(src, dst, send_sem, recv_sem, where):
        return pltpu.make_async_remote_copy(
            src_ref=src, dst_ref=dst, send_sem=send_sem, recv_sem=recv_sem,
            device_id=where, device_id_type=MESH,
        )

    def apart(body):
        pl.when(rep >= 0)(body)

    barrier = pltpu.get_barrier_semaphore()
    partners = (
        [device(dz=o) for o in Z_FAR]
        + [device(dy=d) for d in Y_FAR]
        + [device(dx=ox, dc=oc) for ox, oc in XC_FAR]
    )
    for partner in partners:
        pl.semaphore_signal(barrier, inc=1, device_id=partner, device_id_type=MESH)

    pt_copy = pltpu.make_async_copy(pt_ref, pt_v, pt_sem)
    pt_copy.start()
    a_copies = []
    for k, d in enumerate(RS_ORDER):
        b = ahead[d]
        a_copies.append(pltpu.make_async_copy(a_ref.at[b], a_v.at[b], a_sem.at[k]))
        a_copies[-1].start()

    mine = group_rows(0, 0)
    my_half = pl.ds(pl.multiple_of(c * HALF, HALF), HALF)
    its_half = pl.ds(pl.multiple_of((1 - c) * HALF, HALF), HALF)
    my_x = pl.ds(pl.multiple_of(x * GROUP, GROUP), GROUP)
    sibling = device(dc=1)

    pt_copy.wait()
    for k, d in enumerate(RS_ORDER):
        a_copies[k].wait()
        part[k] = lax.dot_general(
            pt_v[...], a_v[ahead[d]], NT, preferred_element_type=F32
        )
    pl.semaphore_wait(barrier, len(partners))

    def core_copy(i):
        slots = pl.ds(*RS_GROUPS[i])
        return send(part.at[slots, its_half], sib.at[slots], cs, cr.at[i], sibling)

    for i in range(len(RS_GROUPS)):
        core_copy(i).start()
    for i, (first, count) in enumerate(RS_GROUPS):
        slots = pl.ds(first, count)
        core_copy(i).wait_recv()
        half[slots] = part[slots, my_half] + sib[slots]
        for j, o in enumerate(X_FAR):
            rows = pl.ds(pl.multiple_of(lax.rem(x + o, NX) * GROUP, GROUP), GROUP)
            send(
                half.at[slots, rows], xr.at[j, slots], xs, xrs.at[i], device(dx=o)
            ).start()

    def y_copy(k):
        return send(yb.at[k], yr.at[k], ys, yrs, device(dy=RS_ORDER[k]))

    for i, (first, count) in enumerate(RS_GROUPS):
        slots = pl.ds(first, count)
        arrived = xr.at[:, slots]
        send(arrived, arrived, xs, xrs.at[i], sibling).wait_recv()
        for k in range(first, first + count):
            yb[k] = half[k, my_x] + xr[0, k] + xr[1, k] + xr[2, k]
            if k < 7:
                y_copy(k).start()
    send(yr, yr, ys, yrs, sibling).wait_recv()
    total = yb[7]
    for k in range(7):
        total = total + yr[k]

    def z_start(ref, send_sem, recv_sem):
        for o in Z_FAR:
            send(ref.at[z], ref.at[z], send_sem, recv_sem, device(dz=o)).start()

    def z_all(ref, send_sem, recv_sem):
        others = ref.at[pl.ds(0, NZ - 1)]
        return send(others, others, send_sem, recv_sem, sibling)

    def z_sum(ref):
        value = ref[0]
        for i in range(1, NZ):
            value = value + ref[i]
        return value

    zr[z] = total
    z_start(zr, zs, zrs)
    send(part.at[:, its_half], sib, cs, cr.at[0], sibling).wait_send()
    send(xr, xr, xs, xrs.at[0], sibling).wait_send()
    send(yr, yr, ys, yrs, sibling).wait_send()
    z_all(zr, zs, zrs).wait_recv()
    left[0, mine] = z_sum(zr)

    own = left.at[0, mine]
    for d in Y_FAR:
        at = AG_ORDER.index(d)
        group = AG_GROUP_OF[at]
        send(own, left.at[at, mine], ays, ayr.at[group], device(dy=d)).start()
    for i, (first, count) in enumerate(AG_GROUPS):
        slots = pl.ds(first, count)
        arrived = left.at[pl.ds(max(first, 1), count - (first == 0)), mine]
        send(arrived, arrived, ays, ayr.at[i], sibling).wait_recv()
        ref = left.at[slots, mine]
        for o in X_FAR:
            send(ref, ref, axs, axr.at[i], device(dx=o)).start()

    def core_gather(i):
        ref = left.at[pl.ds(*AG_GROUPS[i]), my_half]
        return send(ref, ref, acs, acr.at[i], sibling)

    def contract(i):
        core_gather(i).wait_recv()

        @apart
        def _():
            for k in range(AG_GROUPS[i][0], sum(AG_GROUPS[i])):
                pieces = jnp.concatenate(split3(left[k]), axis=0)
                r = jnp.dot(pieces, a_v[behind[AG_ORDER[k]]], preferred_element_type=F32)
                g = lax.dot_general(pieces, pieces, NT, preferred_element_type=F32)
                if k:
                    racc[...] += r
                    gacc[...] += g
                else:
                    racc[...] = r
                    gacc[...] = g

    for i in range(len(AG_GROUPS)):
        arrived = left.at[pl.ds(*AG_GROUPS[i]), pl.ds(0, 3 * GROUP)]
        send(arrived, arrived, axs, axr.at[i], sibling).wait_recv()
        core_gather(i).start()
        if i:
            contract(i - 1)
    contract(len(AG_GROUPS) - 1)

    rpart[...] = racc[0:64] + racc[64:128] + racc[128:192]
    for i, (ox, oc) in enumerate(XC_FAR):
        send(
            rpart.at[group_rows(ox, oc)], rr.at[i], rs, rrs, device(dx=ox, dc=oc)
        ).start()

    at_row = lax.broadcasted_iota(jnp.int32, (64, 64), 0)
    at_col = lax.broadcasted_iota(jnp.int32, (64, 64), 1)
    diagonal = at_row == at_col

    def steps(first, last):
        tiles = eliminate([both_v[8 * i : 8 * i + 8] for i in range(8)], first, last)
        for i in range(first // 8, 8):
            both_v[8 * i : 8 * i + 8] = tiles[i]

    @apart
    def _():
        one = gacc[0:64, 0:64]
        cross = gacc[0:64, 64:128] + gacc[64:128, 0:64]
        small = gacc[64:128, 64:128] + gacc[0:64, 128:192] + gacc[128:192, 0:64]
        gram = one + (cross + small)
        unit = jnp.where(diagonal, 1.0, 0.0).astype(F32)
        both_v[...] = jnp.concatenate([gram, unit], axis=1)
        steps(0, 16)

    send(rr, rr, rs, rrs, sibling).wait_recv()
    total = rpart[mine]
    for i in range(7):
        total = total + rr[i]
    zr2[z] = total
    z_start(zr2, z2s, z2r)

    @apart
    def _():
        steps(16, 64)
        both = both_v[...]
        scale = jnp.sum(jnp.where(diagonal, both[:, 0:64], 0.0), axis=1, keepdims=True)
        w_v[...] = both[:, 64:128] * (1.0 / jnp.sqrt(scale))

    z_all(zr, zs, zrs).wait_send()
    sent = left.at[pl.ds(0, 7), mine]
    send(sent, sent, ays, ayr.at[0], sibling).wait_send()
    sent = left.at[:, pl.ds(0, 3 * GROUP)]
    send(sent, sent, axs, axr.at[0], sibling).wait_send()
    sent = left.at[:, my_half]
    send(sent, sent, acs, acr.at[0], sibling).wait_send()
    send(rr, rr, rs, rrs, sibling).wait_send()
    z_all(zr2, z2s, z2r).wait_recv()
    rt[mine] = z_sum(zr2)

    ref = rt.at[mine]
    for ox, oc in XC_FAR:
        send(ref, ref, qs, qr, device(dx=ox, dc=oc)).start()

    @apart
    def _():
        for k, d in enumerate(AG_ORDER):
            basis_t = jnp.dot(
                w_v[...], left[k], precision=lax.Precision.HIGHEST, preferred_element_type=F32
            )
            high = basis_t.astype(BF16).astype(F32)
            low = basis_t - high
            packed = jnp.concatenate([high, high, low, low], axis=0)
            bk_ref[behind[d]] = packed.T.astype(BF16)

    z_all(zr2, z2s, z2r).wait_send()
    others = rt.at[pl.ds(0, RANK - GROUP)]
    send(others, others, qs, qr, sibling).wait()
    right_t = jnp.dot(
        w_v[...], rt[...], precision=lax.Precision.HIGHEST, preferred_element_type=F32
    ) * (1.0 / REPS)
    high = right_t.astype(BF16)
    low = (right_t - high.astype(F32)).astype(BF16)
    rk_ref[...] = jnp.concatenate([high, low, high, low], axis=0)


def exchange(prior_t, blocks):
    dma = pltpu.SemaphoreType.DMA
    vmem = pltpu.VMEM
    return pl.pallas_call(
        exchange_kernel,
        out_shape=(
            jax.ShapeDtypeStruct((NY, BLOCK, 4 * RANK), BF16),
            jax.ShapeDtypeStruct((4 * RANK, COLS), BF16),
            jax.ShapeDtypeStruct((NY, BLOCK, COLS), BF16),
        ),
        in_specs=[pl.BlockSpec(memory_space=pltpu.HBM)] * 2,
        out_specs=(pl.BlockSpec(memory_space=pltpu.VMEM),) * 3,
        scratch_shapes=[
            vmem((RANK, BLOCK), BF16),
            vmem((NY, RANK, BLOCK), F32),
            vmem((NY, HALF, BLOCK), F32),
            vmem((NY, HALF, BLOCK), F32),
            vmem((3, NY, GROUP, BLOCK), F32),
            vmem((NY, GROUP, BLOCK), F32),
            vmem((NY - 1, GROUP, BLOCK), F32),
            vmem((NZ, GROUP, BLOCK), F32),
            vmem((NY, RANK, BLOCK), F32),
            vmem((3 * RANK, COLS), F32),
            vmem((3 * RANK, 3 * RANK), F32),
            vmem((RANK, COLS), F32),
            vmem((7, GROUP, COLS), F32),
            vmem((NZ, GROUP, COLS), F32),
            vmem((RANK, COLS), F32),
            vmem((RANK, 2 * RANK), F32),
            vmem((RANK, RANK), F32),
            dma, dma((8,)), dma, dma((4,)),
            dma, dma((4,)),
            dma, dma, dma, dma,
            dma, dma((4,)),
            dma, dma((4,)),
            dma, dma((4,)),
            dma, dma, dma, dma, dma, dma,
        ],
        compiler_params=pltpu.CompilerParams(
            collective_id=0, has_side_effects=True, vmem_limit_bytes=EXCHANGE_VMEM
        ),
        name="exchange",
    )(prior_t, blocks)


def finish_kernel(basis_ref, right_ref, a_ref, update_ref, error_ref, up, er, up_sem, er_sem):
    copies = []
    for b in range(NY):
        decoded = jnp.dot(basis_ref[b], right_ref[...], preferred_element_type=F32)
        up[b] = decoded.astype(BF16)
        copies.append(pltpu.make_async_copy(up.at[b], update_ref.at[b], up_sem.at[b]))
        copies[-1].start()
        er[b] = (a_ref[b].astype(F32) - decoded).astype(BF16)
        copies.append(pltpu.make_async_copy(er.at[b], error_ref.at[b], er_sem.at[b]))
        copies[-1].start()
    for copy in copies:
        copy.wait()


def finish(basis, right, blocks):
    shape = jax.ShapeDtypeStruct(blocks.shape, BF16)
    return pl.pallas_call(
        finish_kernel,
        out_shape=(shape, shape),
        in_specs=[pl.BlockSpec(memory_space=pltpu.VMEM)] * 3,
        out_specs=(pl.BlockSpec(memory_space=pl.ANY),) * 2,
        scratch_shapes=[
            pltpu.VMEM((NY, BLOCK, COLS), BF16),
            pltpu.VMEM((NY, BLOCK, COLS), BF16),
            pltpu.SemaphoreType.DMA((NY,)),
            pltpu.SemaphoreType.DMA((NY,)),
        ],
        compiler_params=pltpu.CompilerParams(vmem_limit_bytes=16 * 2**20),
        name="finish",
    )(basis, right, blocks)


def shards(accumulated, prior_right):
    block = accumulated[0]
    basis, right, held = exchange(prior_right.T, block.reshape(NY, BLOCK, COLS))
    update, error = finish(basis, right, held)
    return update.reshape(block.shape), error.reshape(accumulated.shape)


def solution(mesh):
    placed = (P("rep", None, "shard"), P("shard", None))
    return jax.shard_map(
        shards,
        mesh=mesh,
        in_specs=placed,
        out_specs=(P(None, "shard"), P("rep", None, "shard")),
        check_vma=False,
    )
```

time: 69.8 us -> 68.4 us (0.980)
  Pallas kernels: 68.1 us -> 66.7 us
    pallas_call x1, Pallas kernels: 65.6 us -> 64.2 us  [exchange(): pl.pallas_call(exchange_kernel, out_shape=(jax.ShapeDtypeStruct((NY, BLOC...]
where the time goes in v3:
time: 68.4 us; the launch traced here: 68.2 us
  Pallas kernels  66.7 us (98%)
  local copies, waits for them, and re-layouts  0.79 us (1%)
    pallas_call x1, Pallas kernels, exchange(): pl.pallas_call(exchange_kernel, out_shape=(jax.ShapeDtypeStruct((NY, BLOC...  64.2 us
    pallas_call x1, Pallas kernels, finish(): pl.pallas_call(finish_kernel, out_shape=(shape, shape), in_specs=[pl.Bloc...  2.58 us

profile of v3, /device:TPU:1, one launch (start us, length us, event | category | flops | bytes accessed | tf_op | source)
XLA Modules:
  0.0 68.2 jit_solution(16813672830060533845)
XLA Ops:
  0.6 0.0 copy-start
  0.6 0.8 %copy-done = bf16[384,64]{0,1:T(8,128)(2,1)S(1)} copy-done((bf16[384,64]{0,1:T(8,128)(2,1)S(1)}, bf16[384,64]{0,1:T(8,128)(2,1)}, u32[]{:S(2)}) %copy-start) | copy-done | bytes 49176
  1.4 64.2 %exchange.1 = (bf16[8,384,256]{2,1,0:T(8,128)(2,1)S(1)}, bf16[256,384]{1,0:T(8,128)(2,1)S(1)}, bf16[8,384,384]{2,1,0:T(8,128)(2,1)S(1)}) custom-call(bf16[64,384]{1,0:T(8,128)(2,1)S(1)} %bitcast.4, bf16[8,384,384]{2,1,0:T(8,128)(2,1)} %bitcast.5), custom_call_target="tpu_custom_call" | custom-call | tf_op jit(solution)/shard_map/exchange/pallas_call | solution.py:293
  65.6 2.6 %finish.1 = (bf16[8,384,384]{2,1,0:T(8,128)(2,1)}, bf16[8,384,384]{2,1,0:T(8,128)(2,1)}) custom-call(bf16[8,384,256]{2,1,0:T(8,128)(2,1)S(1)} %get-tuple-element.7.basis_ref, bf16[256,384]{1,0:T(8,128)(2,1)S(1)} %get-tuple-element.8.right_ref, bf16[8,384,384]{2,1,0:T(8,128)(2,1)S(1)} %get-tuple-element.9.a_ref), custom_call_target="tpu_custom_call" | custom-call | tf_op jit(solution)/shard_map/finish/pallas_call | solution.py:351
Async XLA Ops:
  0.6 0.8 %copy-start = (bf16[384,64]{0,1:T(8,128)(2,1)S(1)}, bf16[384,64]{0,1:T(8,128)(2,1)}, u32[]{:S(2)}) copy-start(bf16[384,64]{0,1:T(8,128)(2,1)} %param.3) | copy-start | bytes 147460

commit v4 on v3

--- a/solution.py
+++ b/solution.py
@@ -20,8 +20,8 @@
 RS_ORDER = Y_FAR + (0,)
 RS_GROUPS = ((0, 1), (1, 2), (3, 2), (5, 3))
 AG_ORDER = (0, 1, 7, 2, 6, 3, 5, 4)
-AG_GROUPS = ((0, 3), (3, 2), (5, 2), (7, 1))
-AG_GROUP_OF = (0, 0, 0, 1, 1, 2, 2, 3)
+AG_GROUPS = ((0, 3), (3, 2), (5, 3))
+AG_GROUP_OF = (0, 0, 0, 1, 1, 2, 2, 2)
 Z_FAR = (6, 5, 7, 4, 8, 3, 9, 2, 10, 1, 11)
 XC_FAR = ((2, 1), (2, 0), (1, 1), (3, 1), (1, 0), (3, 0), (0, 1))
 EXCHANGE_VMEM = int(49.95 * 2**20)
@@ -54,7 +54,7 @@
 
 def exchange_kernel(
     pt_ref, a_ref, bk_ref, rk_ref, a_v,
-    pt_v, part, sib, half, xr, yb, yr, zr, left, racc, gacc, rpart, rr, zr2, rt, both_v, w_v,
+    pt_v, part, sib, half, xr, yb, yr, zr, left, pieces_v, racc, gacc, rpart, rr, zr2, rt, both_v, w_v,
     pt_sem, a_sem, cs, cr, xs, xrs, ys, yrs, zs, zrs, ays, ayr, axs, axr, acs, acr,
     rs, rrs, z2s, z2r, qs, qr,
 ):
@@ -194,14 +194,12 @@
         def _():
             for k in range(AG_GROUPS[i][0], sum(AG_GROUPS[i])):
                 pieces = jnp.concatenate(split3(left[k]), axis=0)
+                pieces_v[k] = pieces
                 r = jnp.dot(pieces, a_v[behind[AG_ORDER[k]]], preferred_element_type=F32)
-                g = lax.dot_general(pieces, pieces, NT, preferred_element_type=F32)
                 if k:
                     racc[...] += r
-                    gacc[...] += g
                 else:
                     racc[...] = r
-                    gacc[...] = g
 
     for i in range(len(AG_GROUPS)):
         arrived = left.at[pl.ds(*AG_GROUPS[i]), pl.ds(0, 3 * GROUP)]
@@ -228,13 +226,20 @@
 
     @apart
     def _():
+        for k in range(NY):
+            pieces = pieces_v[k]
+            g = lax.dot_general(pieces, pieces, NT, preferred_element_type=F32)
+            if k:
+                gacc[...] += g
+            else:
+                gacc[...] = g
         one = gacc[0:64, 0:64]
         cross = gacc[0:64, 64:128] + gacc[64:128, 0:64]
         small = gacc[64:128, 64:128] + gacc[0:64, 128:192] + gacc[128:192, 0:64]
         gram = one + (cross + small)
         unit = jnp.where(diagonal, 1.0, 0.0).astype(F32)
         both_v[...] = jnp.concatenate([gram, unit], axis=1)
-        steps(0, 16)
+        steps(0, 12)
 
     send(rr, rr, rs, rrs, sibling).wait_recv()
     total = rpart[mine]
@@ -245,7 +250,7 @@
 
     @apart
     def _():
-        steps(16, 64)
+        steps(12, 64)
         both = both_v[...]
         scale = jnp.sum(jnp.where(diagonal, both[:, 0:64], 0.0), axis=1, keepdims=True)
         w_v[...] = both[:, 64:128] * (1.0 / jnp.sqrt(scale))
@@ -309,6 +314,7 @@
             vmem((NY - 1, GROUP, BLOCK), F32),
             vmem((NZ, GROUP, BLOCK), F32),
             vmem((NY, RANK, BLOCK), F32),
+            vmem((NY, 3 * RANK, BLOCK), BF16),
             vmem((3 * RANK, COLS), F32),
             vmem((3 * RANK, 3 * RANK), F32),
             vmem((RANK, COLS), F32),

time: 68.4 us -> 67.8 us (level)
  no operation moved by 1% of the time
where the time goes in v4:
time: 67.8 us; the launch traced here: 67.6 us
  Pallas kernels  66.1 us (97%)
  local copies, waits for them, and re-layouts  0.79 us (1%)
    pallas_call x1, Pallas kernels, exchange(): pl.pallas_call(exchange_kernel, out_shape=(jax.ShapeDtypeStruct((NY, BLOC...  63.5 us
    pallas_call x1, Pallas kernels, finish(): pl.pallas_call(finish_kernel, out_shape=(shape, shape), in_specs=[pl.Bloc...  2.58 us

profile of v4, /device:TPU:1, one launch (start us, length us, event | category | flops | bytes accessed | tf_op | source)
XLA Modules:
  0.0 67.6 jit_solution(3824502099316822413)
XLA Ops:
  0.6 0.0 copy-start
  0.6 0.8 %copy-done = bf16[384,64]{0,1:T(8,128)(2,1)S(1)} copy-done((bf16[384,64]{0,1:T(8,128)(2,1)S(1)}, bf16[384,64]{0,1:T(8,128)(2,1)}, u32[]{:S(2)}) %copy-start) | copy-done | bytes 49176
  1.4 63.5 %exchange.1 = (bf16[8,384,256]{2,1,0:T(8,128)(2,1)S(1)}, bf16[256,384]{1,0:T(8,128)(2,1)S(1)}, bf16[8,384,384]{2,1,0:T(8,128)(2,1)S(1)}) custom-call(bf16[64,384]{1,0:T(8,128)(2,1)S(1)} %bitcast.4, bf16[8,384,384]{2,1,0:T(8,128)(2,1)} %bitcast.5), custom_call_target="tpu_custom_call" | custom-call | tf_op jit(solution)/shard_map/exchange/pallas_call | solution.py:298
  65.0 2.6 %finish.1 = (bf16[8,384,384]{2,1,0:T(8,128)(2,1)}, bf16[8,384,384]{2,1,0:T(8,128)(2,1)}) custom-call(bf16[8,384,256]{2,1,0:T(8,128)(2,1)S(1)} %get-tuple-element.7.basis_ref, bf16[256,384]{1,0:T(8,128)(2,1)S(1)} %get-tuple-element.8.right_ref, bf16[8,384,384]{2,1,0:T(8,128)(2,1)S(1)} %get-tuple-element.9.a_ref), custom_call_target="tpu_custom_call" | custom-call | tf_op jit(solution)/shard_map/finish/pallas_call | solution.py:357
Async XLA Ops:
  0.6 0.8 %copy-start = (bf16[384,64]{0,1:T(8,128)(2,1)S(1)}, bf16[384,64]{0,1:T(8,128)(2,1)}, u32[]{:S(2)}) copy-start(bf16[384,64]{0,1:T(8,128)(2,1)} %param.3) | copy-start | bytes 147460

commit v5 on v4

--- a/solution.py
+++ b/solution.py
@@ -20,8 +20,10 @@
 RS_ORDER = Y_FAR + (0,)
 RS_GROUPS = ((0, 1), (1, 2), (3, 2), (5, 3))
 AG_ORDER = (0, 1, 7, 2, 6, 3, 5, 4)
-AG_GROUPS = ((0, 3), (3, 2), (5, 3))
-AG_GROUP_OF = (0, 0, 0, 1, 1, 2, 2, 2)
+AG_GROUPS = ((0, 3), (3, 2), (5, 2))
+CORE_GROUPS = ((0, 3), (3, 2), (5, 3))
+AG_GROUP_OF = (0, 0, 0, 1, 1, 2, 2, 3)
+ACROSS = 4
 Z_FAR = (6, 5, 7, 4, 8, 3, 9, 2, 10, 1, 11)
 XC_FAR = ((2, 1), (2, 0), (1, 1), (3, 1), (1, 0), (3, 0), (0, 1))
 EXCHANGE_VMEM = int(49.95 * 2**20)
@@ -90,6 +92,7 @@
         [device(dz=o) for o in Z_FAR]
         + [device(dy=d) for d in Y_FAR]
         + [device(dx=ox, dc=oc) for ox, oc in XC_FAR]
+        + [device(dx=o, dy=ACROSS) for o in X_FAR]
     )
     for partner in partners:
         pl.semaphore_signal(barrier, inc=1, device_id=partner, device_id_type=MESH)
@@ -126,8 +129,15 @@
         slots = pl.ds(first, count)
         core_copy(i).wait_recv()
         half[slots] = part[slots, my_half] + sib[slots]
+        if i == 0:
+            send(half.at[0, my_x], yr.at[0], ys, yrs, device(dy=ACROSS)).start()
         for j, o in enumerate(X_FAR):
             rows = pl.ds(pl.multiple_of(lax.rem(x + o, NX) * GROUP, GROUP), GROUP)
+            if i == 0:
+                send(
+                    half.at[0, rows], yr.at[7 + j], ys, yrs, device(dx=o, dy=ACROSS)
+                ).start()
+                continue
             send(
                 half.at[slots, rows], xr.at[j, slots], xs, xrs.at[i], device(dx=o)
             ).start()
@@ -136,6 +146,8 @@
         return send(yb.at[k], yr.at[k], ys, yrs, device(dy=RS_ORDER[k]))
 
     for i, (first, count) in enumerate(RS_GROUPS):
+        if i == 0:
+            continue
         slots = pl.ds(first, count)
         arrived = xr.at[:, slots]
         send(arrived, arrived, xs, xrs.at[i], sibling).wait_recv()
@@ -145,7 +157,7 @@
                 y_copy(k).start()
     send(yr, yr, ys, yrs, sibling).wait_recv()
     total = yb[7]
-    for k in range(7):
+    for k in range(10):
         total = total + yr[k]
 
     def z_start(ref, send_sem, recv_sem):
@@ -165,7 +177,8 @@
     zr[z] = total
     z_start(zr, zs, zrs)
     send(part.at[:, its_half], sib, cs, cr.at[0], sibling).wait_send()
-    send(xr, xr, xs, xrs.at[0], sibling).wait_send()
+    passed = xr.at[:, pl.ds(1, NY - 1)]
+    send(passed, passed, xs, xrs.at[0], sibling).wait_send()
     send(yr, yr, ys, yrs, sibling).wait_send()
     z_all(zr, zs, zrs).wait_recv()
     left[0, mine] = z_sum(zr)
@@ -175,6 +188,9 @@
         at = AG_ORDER.index(d)
         group = AG_GROUP_OF[at]
         send(own, left.at[at, mine], ays, ayr.at[group], device(dy=d)).start()
+        if d == ACROSS:
+            for o in X_FAR:
+                send(own, left.at[at, mine], ays, axr.at[group], device(dx=o, dy=d)).start()
     for i, (first, count) in enumerate(AG_GROUPS):
         slots = pl.ds(first, count)
         arrived = left.at[pl.ds(max(first, 1), count - (first == 0)), mine]
@@ -184,7 +200,7 @@
             send(ref, ref, axs, axr.at[i], device(dx=o)).start()
 
     def core_gather(i):
-        ref = left.at[pl.ds(*AG_GROUPS[i]), my_half]
+        ref = left.at[pl.ds(*CORE_GROUPS[i]), my_half]
         return send(ref, ref, acs, acr.at[i], sibling)
 
     def contract(i):
@@ -192,7 +208,7 @@
 
         @apart
         def _():
-            for k in range(AG_GROUPS[i][0], sum(AG_GROUPS[i])):
+            for k in range(CORE_GROUPS[i][0], sum(CORE_GROUPS[i])):
                 pieces = jnp.concatenate(split3(left[k]), axis=0)
                 pieces_v[k] = pieces
                 r = jnp.dot(pieces, a_v[behind[AG_ORDER[k]]], preferred_element_type=F32)
@@ -204,6 +220,11 @@
     for i in range(len(AG_GROUPS)):
         arrived = left.at[pl.ds(*AG_GROUPS[i]), pl.ds(0, 3 * GROUP)]
         send(arrived, arrived, axs, axr.at[i], sibling).wait_recv()
+        if i == len(AG_GROUPS) - 1:
+            arrived = left.at[NY - 1, mine]
+            send(arrived, arrived, ays, ayr.at[i + 1], sibling).wait_recv()
+            arrived = left.at[NY - 1, pl.ds(0, 3 * GROUP)]
+            send(arrived, arrived, ays, axr.at[i + 1], sibling).wait_recv()
         core_gather(i).start()
         if i:
             contract(i - 1)
@@ -256,9 +277,8 @@
         w_v[...] = both[:, 64:128] * (1.0 / jnp.sqrt(scale))
 
     z_all(zr, zs, zrs).wait_send()
-    sent = left.at[pl.ds(0, 7), mine]
-    send(sent, sent, ays, ayr.at[0], sibling).wait_send()
-    sent = left.at[:, pl.ds(0, 3 * GROUP)]
+    send(yr, yr, ays, ayr.at[0], sibling).wait_send()
+    sent = left.at[pl.ds(0, 7), pl.ds(0, 3 * GROUP)]
     send(sent, sent, axs, axr.at[0], sibling).wait_send()
     sent = left.at[:, my_half]
     send(sent, sent, acs, acr.at[0], sibling).wait_send()
@@ -311,7 +331,7 @@
             vmem((NY, HALF, BLOCK), F32),
             vmem((3, NY, GROUP, BLOCK), F32),
             vmem((NY, GROUP, BLOCK), F32),
-            vmem((NY - 1, GROUP, BLOCK), F32),
+            vmem((NY + 2, GROUP, BLOCK), F32),
             vmem((NZ, GROUP, BLOCK), F32),
             vmem((NY, RANK, BLOCK), F32),
             vmem((NY, 3 * RANK, BLOCK), BF16),

time: 67.8 us -> 70.2 us (1.035)
  Pallas kernels: 66.1 us -> 68.5 us
    pallas_call x1, Pallas kernels: 63.5 us -> 65.9 us  [exchange(): pl.pallas_call(exchange_kernel, out_shape=(jax.ShapeDtypeStruct((NY, BLOC...]
where the time goes in v5:
time: 70.2 us; the launch traced here: 69.9 us
  Pallas kernels  68.5 us (98%)
  local copies, waits for them, and re-layouts  0.79 us (1%)
    pallas_call x1, Pallas kernels, exchange(): pl.pallas_call(exchange_kernel, out_shape=(jax.ShapeDtypeStruct((NY, BLOC...  65.9 us
    pallas_call x1, Pallas kernels, finish(): pl.pallas_call(finish_kernel, out_shape=(shape, shape), in_specs=[pl.Bloc...  2.58 us

profile of v5, /device:TPU:1, one launch (start us, length us, event | category | flops | bytes accessed | tf_op | source)
XLA Modules:
  0.0 69.9 jit_solution(13864485814049678783)
XLA Ops:
  0.6 0.0 copy-start
  0.6 0.8 %copy-done = bf16[384,64]{0,1:T(8,128)(2,1)S(1)} copy-done((bf16[384,64]{0,1:T(8,128)(2,1)S(1)}, bf16[384,64]{0,1:T(8,128)(2,1)}, u32[]{:S(2)}) %copy-start) | copy-done | bytes 49176
  1.4 65.9 %exchange.1 = (bf16[8,384,256]{2,1,0:T(8,128)(2,1)S(1)}, bf16[256,384]{1,0:T(8,128)(2,1)S(1)}, bf16[8,384,384]{2,1,0:T(8,128)(2,1)S(1)}) custom-call(bf16[64,384]{1,0:T(8,128)(2,1)S(1)} %bitcast.4, bf16[8,384,384]{2,1,0:T(8,128)(2,1)} %bitcast.5), custom_call_target="tpu_custom_call" | custom-call | tf_op jit(solution)/shard_map/exchange/pallas_call | solution.py:318
  67.4 2.6 %finish.1 = (bf16[8,384,384]{2,1,0:T(8,128)(2,1)}, bf16[8,384,384]{2,1,0:T(8,128)(2,1)}) custom-call(bf16[8,384,256]{2,1,0:T(8,128)(2,1)S(1)} %get-tuple-element.7.basis_ref, bf16[256,384]{1,0:T(8,128)(2,1)S(1)} %get-tuple-element.8.right_ref, bf16[8,384,384]{2,1,0:T(8,128)(2,1)S(1)} %get-tuple-element.9.a_ref), custom_call_target="tpu_custom_call" | custom-call | tf_op jit(solution)/shard_map/finish/pallas_call | solution.py:377
Async XLA Ops:
  0.6 0.8 %copy-start = (bf16[384,64]{0,1:T(8,128)(2,1)S(1)}, bf16[384,64]{0,1:T(8,128)(2,1)}, u32[]{:S(2)}) copy-start(bf16[384,64]{0,1:T(8,128)(2,1)} %param.3) | copy-start | bytes 147460

commit v6 on v4

--- a/solution.py
+++ b/solution.py
@@ -54,8 +54,8 @@
 
 def exchange_kernel(
     pt_ref, a_ref, bk_ref, rk_ref, a_v,
-    pt_v, part, sib, half, xr, yb, yr, zr, left, pieces_v, racc, gacc, rpart, rr, zr2, rt, both_v, w_v,
-    pt_sem, a_sem, cs, cr, xs, xrs, ys, yrs, zs, zrs, ays, ayr, axs, axr, acs, acr,
+    part, sib, half, xr, yb, yr, zr, left, pieces_v, racc, gacc, rpart, rr, zr2, rt, both_v, w_v,
+    a_sem, cs, cr, xs, xrs, ys, yrs, zs, zrs, ays, ayr, axs, axr, acs, acr,
     rs, rrs, z2s, z2r, qs, qr,
 ):
     rep, y = lax.axis_index("rep"), lax.axis_index("shard")
@@ -94,8 +94,6 @@
     for partner in partners:
         pl.semaphore_signal(barrier, inc=1, device_id=partner, device_id_type=MESH)
 
-    pt_copy = pltpu.make_async_copy(pt_ref, pt_v, pt_sem)
-    pt_copy.start()
     a_copies = []
     for k, d in enumerate(RS_ORDER):
         b = ahead[d]
@@ -108,11 +106,10 @@
     my_x = pl.ds(pl.multiple_of(x * GROUP, GROUP), GROUP)
     sibling = device(dc=1)
 
-    pt_copy.wait()
     for k, d in enumerate(RS_ORDER):
         a_copies[k].wait()
         part[k] = lax.dot_general(
-            pt_v[...], a_v[ahead[d]], NT, preferred_element_type=F32
+            pt_ref[...], a_v[ahead[d]], NT, preferred_element_type=F32
         )
     pl.semaphore_wait(barrier, len(partners))
 
@@ -192,14 +189,15 @@
 
         @apart
         def _():
+            r = racc[...] if i else 0.0
             for k in range(AG_GROUPS[i][0], sum(AG_GROUPS[i])):
                 pieces = jnp.concatenate(split3(left[k]), axis=0)
                 pieces_v[k] = pieces
-                r = jnp.dot(pieces, a_v[behind[AG_ORDER[k]]], preferred_element_type=F32)
-                if k:
-                    racc[...] += r
-                else:
-                    racc[...] = r
+                r += jnp.dot(pieces, a_v[behind[AG_ORDER[k]]], preferred_element_type=F32)
+            if i < len(AG_GROUPS) - 1:
+                racc[...] = r
+            else:
+                rpart[...] = r[0:64] + r[64:128] + r[128:192]
 
     for i in range(len(AG_GROUPS)):
         arrived = left.at[pl.ds(*AG_GROUPS[i]), pl.ds(0, 3 * GROUP)]
@@ -209,7 +207,6 @@
             contract(i - 1)
     contract(len(AG_GROUPS) - 1)
 
-    rpart[...] = racc[0:64] + racc[64:128] + racc[128:192]
     for i, (ox, oc) in enumerate(XC_FAR):
         send(
             rpart.at[group_rows(ox, oc)], rr.at[i], rs, rrs, device(dx=ox, dc=oc)
@@ -302,10 +299,12 @@
             jax.ShapeDtypeStruct((4 * RANK, COLS), BF16),
             jax.ShapeDtypeStruct((NY, BLOCK, COLS), BF16),
         ),
-        in_specs=[pl.BlockSpec(memory_space=pltpu.HBM)] * 2,
+        in_specs=[
+            pl.BlockSpec(memory_space=pltpu.VMEM),
+            pl.BlockSpec(memory_space=pltpu.HBM),
+        ],
         out_specs=(pl.BlockSpec(memory_space=pltpu.VMEM),) * 3,
         scratch_shapes=[
-            vmem((RANK, BLOCK), BF16),
             vmem((NY, RANK, BLOCK), F32),
             vmem((NY, HALF, BLOCK), F32),
             vmem((NY, HALF, BLOCK), F32),
@@ -323,7 +322,7 @@
             vmem((RANK, COLS), F32),
             vmem((RANK, 2 * RANK), F32),
             vmem((RANK, RANK), F32),
-            dma, dma((8,)), dma, dma((4,)),
+            dma((8,)), dma, dma((4,)),
             dma, dma((4,)),
             dma, dma, dma, dma,
             dma, dma((4,)),

time: 67.8 us -> 67.7 us (level)
  no operation moved by 1% of the time
where the time goes in v6:
time: 67.7 us; the launch traced here: 67.5 us
  Pallas kernels  66.1 us (98%)
  local copies, waits for them, and re-layouts  0.79 us (1%)
    pallas_call x1, Pallas kernels, exchange(): pl.pallas_call(exchange_kernel, out_shape=(jax.ShapeDtypeStruct((NY, BLOC...  63.5 us
    pallas_call x1, Pallas kernels, finish(): pl.pallas_call(finish_kernel, out_shape=(shape, shape), in_specs=[pl.Bloc...  2.58 us

profile of v6, /device:TPU:1, one launch (start us, length us, event | category | flops | bytes accessed | tf_op | source)
XLA Modules:
  0.0 67.5 jit_solution(13658877488337618407)
XLA Ops:
  0.6 0.0 copy-start
  0.6 0.8 %copy-done = bf16[384,64]{0,1:T(8,128)(2,1)S(1)} copy-done((bf16[384,64]{0,1:T(8,128)(2,1)S(1)}, bf16[384,64]{0,1:T(8,128)(2,1)}, u32[]{:S(2)}) %copy-start) | copy-done | bytes 49176
  1.4 63.5 %exchange.1 = (bf16[8,384,256]{2,1,0:T(8,128)(2,1)S(1)}, bf16[256,384]{1,0:T(8,128)(2,1)S(1)}, bf16[8,384,384]{2,1,0:T(8,128)(2,1)S(1)}) custom-call(bf16[64,384]{1,0:T(8,128)(2,1)S(1)} %bitcast.4, bf16[8,384,384]{2,1,0:T(8,128)(2,1)} %bitcast.5), custom_call_target="tpu_custom_call" | custom-call | tf_op jit(solution)/shard_map/exchange/pallas_call | solution.py:295
  64.9 2.6 %finish.1 = (bf16[8,384,384]{2,1,0:T(8,128)(2,1)}, bf16[8,384,384]{2,1,0:T(8,128)(2,1)}) custom-call(bf16[8,384,256]{2,1,0:T(8,128)(2,1)S(1)} %get-tuple-element.7.basis_ref, bf16[256,384]{1,0:T(8,128)(2,1)S(1)} %get-tuple-element.8.right_ref, bf16[8,384,384]{2,1,0:T(8,128)(2,1)S(1)} %get-tuple-element.9.a_ref), custom_call_target="tpu_custom_call" | custom-call | tf_op jit(solution)/shard_map/finish/pallas_call | solution.py:356
Async XLA Ops:
  0.6 0.8 %copy-start = (bf16[384,64]{0,1:T(8,128)(2,1)S(1)}, bf16[384,64]{0,1:T(8,128)(2,1)}, u32[]{:S(2)}) copy-start(bf16[384,64]{0,1:T(8,128)(2,1)} %param.3) | copy-start | bytes 147460
